TPU v7x, 32 devices: a whole 2x2x4 slice. The times are simulated.
32 devices in a mesh: gz: 2 (over y), gy: 4 (over x, core), gx: 4 (over z).
Axes of the slice: x: 2, y: 2, z: 4, core: 2. Of those that a mesh axis runs over, the one named last changes fastest.
Arguments:
- labels: int32 [2, 32, 512], P('gz', 'gy', 'gx'), may hold values from 0 to 7
- tissue_tensors: float32 [6, 8], replicated, as said below
- electrodes: int32 [2, 64], replicated, may hold values from 0 to 32767, as said below
- initial: float32 [64, 2, 32, 512], P(None, 'gz', 'gy', 'gx'), may hold values from -4 to 4
Outputs:
- solution: float32 [64, 2, 32, 512], P(None, 'gz', 'gy', 'gx')
- residual: float32 [64, 2, 32, 512], P(None, 'gz', 'gy', 'gx')
Inputs may be any that keep to these rules, and one draw needn't show every extreme that they name: `tissue_tensors`: the tensors are symmetric and positive definite: each off-diagonal component is at most 0.3 times the geometric mean of its two diagonal components. `electrodes`: all 128 voxel indices are distinct; voxel (z, y, x) has index (z * 32 + y) * 512 + x.
All inputs are finite; a program needn't handle non-finite values.
Results may differ from a plain program's by a relative error of at most 0.0003.
Values sent between devices are 32-bit elements; how exact they have to be, the bound alone decides.
A program may use at most 64 MiB of HBM per device.

v0:
```python
import jax
import jax.numpy as jnp
from jax import lax
from jax.sharding import PartitionSpec as P

ITERS = 2


def from_behind(value, axis, steps):
    count = lax.axis_size(axis)
    initial, last = (max(0, -steps), min(count, count - steps))
    return lax.ppermute(value, axis, [(source, source + steps) for source in range(initial, last)])


def padded_2(block, sides, width):
    for axis, dim in sides:
        count = lax.axis_size(axis)
        forward = [(i, i + 1) for i in range(count - 1)]
        backward = [(target, source) for source, target in forward]
        low = lax.ppermute(
            lax.slice_in_dim(block, block.shape[dim] - width, None, axis=dim), axis, forward
        )
        high = lax.ppermute(lax.slice_in_dim(block, 0, width, axis=dim), axis, backward)
        block = jnp.concatenate([low, block, high], axis=dim)
    return block


def tensor_lookup(labels, table):
    result = jnp.zeros((6,) + labels.shape, jnp.float32)
    for tissue in range(table.shape[1]):
        result = result + jnp.where(
            labels[None] == tissue, table[:, tissue][:, None, None, None], jnp.float32(0.0)
        )
    return result


def flux_terms(tensor, grad_x, grad_y, grad_z):
    flux_x = tensor[0] * grad_x + tensor[3] * grad_y + tensor[4] * grad_z
    flux_y = tensor[3] * grad_x + tensor[1] * grad_y + tensor[5] * grad_z
    flux_z = tensor[4] * grad_x + tensor[5] * grad_y + tensor[2] * grad_z
    return (flux_x, flux_y, flux_z)


def lower_box(tensor):
    below_z = from_behind(tensor, "gz", 1)
    below_y = from_behind(tensor[:, :, -1:], "gy", 1)
    below_x = from_behind(tensor[:, :, :, -1:], "gx", 1)
    inner = jnp.concatenate([below_x, tensor], axis=3)
    side_y = jnp.pad(below_y, ((0, 0), (0, 0), (0, 0), (1, 0)))
    inner = jnp.concatenate([side_y, inner], axis=2)
    side_z = jnp.pad(below_z, ((0, 0), (0, 0), (1, 0), (1, 0)))
    return jnp.concatenate([side_z, inner], axis=1)


def operate_faces(direction, tensor_box):
    padded = padded_2(direction, (("gz", 1), ("gy", 2), ("gx", 3)), 1)
    centre = padded[:, :-1, :-1, :-1]
    grad_z = padded[:, 1:, :-1, :-1] - centre
    grad_y = padded[:, :-1, 1:, :-1] - centre
    grad_x = padded[:, :-1, :-1, 1:] - centre
    flux_x, flux_y, flux_z = flux_terms(tensor_box, grad_x, grad_y, grad_z)
    return (
        flux_z[:, :-1, 1:, 1:]
        - flux_z[:, 1:, 1:, 1:]
        + (flux_y[:, 1:, :-1, 1:] - flux_y[:, 1:, 1:, 1:])
        + (flux_x[:, 1:, 1:, :-1] - flux_x[:, 1:, 1:, 1:])
    )


def gram_of(first, second):
    leads = first.shape[0]
    return lax.dot_general(
        first.reshape(leads, -1),
        second.reshape(leads, -1),
        (((1,), (1,)), ((), ())),
        precision=lax.Precision.HIGHEST,
        preferred_element_type=jnp.float32,
    )


def combine_rows(coef, field):
    leads = field.shape[0]
    return jnp.dot(
        coef.T,
        field.reshape(leads, -1),
        precision=lax.Precision.HIGHEST,
        preferred_element_type=jnp.float32,
    ).reshape(field.shape)


def factor_solve(matrix, target):
    factor = jnp.linalg.cholesky(matrix)
    halfway = lax.linalg.triangular_solve(factor, target, left_side=True, lower=True)
    return lax.linalg.triangular_solve(
        factor, halfway, left_side=True, lower=True, transpose_a=True
    )


def body(labels, tissue_tensors, electrodes, initial):
    cells_z, cells_y, cells_x = labels.shape
    rows_all = cells_y * lax.axis_size("gy")
    cols_all = cells_x * lax.axis_size("gx")
    depth_ids = lax.axis_index("gz") * cells_z + lax.broadcasted_iota(jnp.int32, labels.shape, 0)
    row_ids = lax.axis_index("gy") * cells_y + lax.broadcasted_iota(jnp.int32, labels.shape, 1)
    col_ids = lax.axis_index("gx") * cells_x + lax.broadcasted_iota(jnp.int32, labels.shape, 2)
    voxel_id = (depth_ids * rows_all + row_ids) * cols_all + col_ids
    sources = (voxel_id[None] == electrodes[0][:, None, None, None]).astype(jnp.float32) - (
        voxel_id[None] == electrodes[1][:, None, None, None]
    ).astype(jnp.float32)
    tensor = tensor_lookup(labels, tissue_tensors)
    tensor_box = lower_box(tensor)

    def operate(field):
        return operate_faces(field, tensor_box)

    solution = initial
    residual = sources - operate(initial)
    direction = residual
    rr_now = lax.psum(gram_of(residual, residual), ("gz", "gy", "gx"))
    for iteration in range(ITERS):
        image = operate(direction)
        curve = lax.psum(gram_of(direction, image), ("gz", "gy", "gx"))
        step_coef = factor_solve(curve, rr_now)
        solution = solution + combine_rows(step_coef, direction)
        residual = residual - combine_rows(step_coef, image)
        if iteration + 1 < ITERS:
            rr_next = lax.psum(gram_of(residual, residual), ("gz", "gy", "gx"))
            beta_coef = factor_solve(rr_now, rr_next)
            direction = residual + combine_rows(beta_coef, direction)
            rr_now = rr_next
    return (solution, residual)


def solution(mesh):
    placed = (P("gz", "gy", "gx"), P(), P(), P(None, "gz", "gy", "gx"))
    return jax.shard_map(
        body,
        mesh=mesh,
        in_specs=placed,
        out_specs=(P(None, "gz", "gy", "gx"), P(None, "gz", "gy", "gx")),
        check_vma=False,
    )
```

profile of v0, /device:TPU:0, one launch (start us, length us, event | category | flops | bytes accessed | tf_op | source)
XLA Modules:
  0.0 279.7 jit_solution(1200948065979888118)
XLA Ops:
  1.7 4.9 %collective-permute-start.3 = (f32[64,1,8,128]{3,0,2,1:T(8,128)S(1)}, f32[64,1,8,128]{3,0,2,1:T(8,128)S(1)}, u32[]{:S(2)}, u32[]{:S(2)}) collective-permute-start(f32[64,1,8,128]{3,0,2,1:T(8,128)S(1)} %copy.64), channel_id=1, source_target_pairs={{0,16},{1,17},{2,18},{3,19},{4,20},{5,21},{6,22},{7,23},{8,24},{9,... | collective-permute-start | bytes 786440 | tf_op jit(solution)/shard_map/ppermute | solution.py:20
  10.0 4.6 %collective-permute-start = (f32[6,1,8,128]{3,2,1,0:T(8,128)S(1)}, f32[6,1,8,128]{3,2,1,0:T(8,128)S(1)}, u32[]{:S(2)}, u32[]{:S(2)}) collective-permute-start(f32[6,1,8,128]{3,2,1,0:T(8,128)S(1)} %select_add_fusion), channel_id=1, source_target_pairs={{0,16},{1,17},{2,18},{3,19},{4,20},{5,21},{6,22},{7,23},{8,24},{9,... | collective-permute-start | bytes 73736 | tf_op jit(solution)/shard_map/ppermute | solution.py:12
  14.6 3.5 %collective-permute-start.2 = (f32[6,1,8,1]{3,2,1,0:T(8,128)S(1)}, f32[6,1,8,1]{3,2,1,0:T(8,128)S(1)}, u32[]{:S(2)}, u32[]{:S(2)}) collective-permute-start(f32[6,1,8,1]{3,2,1,0:T(8,128)S(1)} %slice.282), channel_id=1, source_target_pairs={{0,1},{1,2},{2,3},{4,5},{5,6},{6,7},{8,9},{9,10},{10,11},{12,13},{... | collective-permute-start | bytes 584 | tf_op jit(solution)/shard_map/ppermute | solution.py:12
  20.4 4.1 %collective-permute-start.5 = (f32[64,3,1,128]{3,0,2,1:T(8,128)S(1)}, f32[64,3,1,128]{3,0,2,1:T(8,128)S(1)}, u32[]{:S(2)}, u32[]{:S(2)}) collective-permute-start(f32[64,3,1,128]{3,0,2,1:T(8,128)S(1)} %get-tuple-element.43), channel_id=1, source_target_pairs={{0,4},{4,8},{8,12},{1,5},{5,9},{9,13},{2,6},{6,10},{10,14},{3,7},{... | collective-permute-start | bytes 294920 | tf_op jit(solution)/shard_map/ppermute | solution.py:20
  29.2 3.5 %collective-permute-start.8 = (f32[64,3,10,1]{0,3,2,1:T(1,128)}, f32[64,3,10,1]{0,3,2,1:T(1,128)S(1)}, u32[]{:S(2)}, u32[]{:S(2)}) collective-permute-start(f32[64,3,10,1]{0,3,2,1:T(1,128)} %copy.52), channel_id=1, source_target_pairs={{0,1},{1,2},{2,3},{4,5},{5,6},{6,7},{8,9},{9,10},{10,11},{12,13},{... | collective-permute-start | bytes 23048 | tf_op jit(solution)/shard_map/ppermute | solution.py:20
  44.5 4.6 %collective-permute-start.9 = (f32[64,1,8,128]{3,0,2,1:T(8,128)S(1)}, f32[64,1,8,128]{3,0,2,1:T(8,128)S(1)}, u32[]{:S(2)}, u32[]{:S(2)}) collective-permute-start(f32[64,1,8,128]{3,0,2,1:T(8,128)S(1)} %fusion.21), channel_id=1, source_target_pairs={{0,16},{1,17},{2,18},{3,19},{4,20},{5,21},{6,22},{7,23},{8,24},{9,... | collective-permute-start | bytes 786440 | tf_op jit(solution)/shard_map/ppermute | solution.py:20
  49.1 4.9 %collective-permute-done.10 = f32[64,1,8,128]{3,0,2,1:T(8,128)S(1)} collective-permute-done((f32[64,1,8,128]{3,0,2,1:T(8,128)S(1)}, f32[64,1,8,128]{3,0,2,1:T(8,128)S(1)}, u32[]{:S(2)}, u32[]{:S(2)}) %collective-permute-start.10) | collective-permute-done | bytes 262176 | tf_op jit(solution)/shard_map/ppermute | solution.py:23
  55.7 2.2 collective-permute-start.11
  61.8 3.4 %collective-permute-start.14 = (f32[64,3,10,1]{0,3,2,1:T(1,128)S(1)}, f32[64,3,10,1]{0,3,2,1:T(1,128)S(1)}, u32[]{:S(2)}, u32[]{:S(2)}) collective-permute-start(f32[64,3,10,1]{0,3,2,1:T(1,128)S(1)} %copy.56), channel_id=1, source_target_pairs={{0,1},{1,2},{2,3},{4,5},{5,6},{6,7},{8,9},{9,10},{10,11},{12,13},{... | collective-permute-start | bytes 23048 | tf_op jit(solution)/shard_map/ppermute | solution.py:20
  73.3 2.0 copy.55
  78.5 42.6 %all-reduce.2 = (f32[64,64]{0,1:T(8,128)S(1)}, f32[64,64]{0,1:T(8,128)S(1)}) all-reduce(f32[64,64]{0,1:T(8,128)S(1)} %copy-done.22, f32[64,64]{0,1:T(8,128)S(1)} %convolution_bitcast_fusion.11), channel_id=1, replica_groups=mesh['gz'=2,'gy'=4,'gx'=4] {'gz','gy','gx'}, use_global_device_ids=true, to_apply=%region_3.5 | all-reduce | flops 8192 | bytes 65536 | tf_op jit(solution)/shard_map/psum | solution.py:119
  121.3 5.8 %cholesky.70 = f32[64,64]{1,0:T(8,128)S(1)} custom-call(f32[64,64]{1,0:T(8,128)S(1)} %get-tuple-element.61), custom_call_target="Cholesky" | custom-call | tf_op jit(solution)/shard_map/jit(cholesky)/cholesky | solution.py:92
  128.5 4.9 %custom-call.15 = f32[1,64,64]{1,2,0:T(8,128)S(1)} custom-call(f32[1,64,64]{2,1,0:T(8,128)S(1)} %fusion.34), custom_call_target="InvertDiagBlocksLowerTriangular" | custom-call | tf_op jit(solution)/shard_map/triangular_solve/custom-call.2 | solution.py:94
  133.4 5.9 %cholesky.59 = f32[64,64]{1,0:T(8,128)S(1)} custom-call(f32[64,64]{1,0:T(8,128)S(1)} %get-tuple-element.62), custom_call_target="Cholesky" | custom-call | tf_op jit(solution)/shard_map/jit(cholesky)/cholesky | solution.py:92
  140.6 4.9 %custom-call.13 = f32[1,64,64]{1,2,0:T(8,128)S(1)} custom-call(f32[1,64,64]{2,1,0:T(8,128)S(1)} %fusion.33), custom_call_target="InvertDiagBlocksLowerTriangular" | custom-call | tf_op jit(solution)/shard_map/triangular_solve/custom-call.2 | solution.py:94
  146.8 38.9 %psum.30 = f32[64,64]{1,0:T(8,128)S(1)} all-reduce(f32[64,64]{1,0:T(8,128)S(1)} %convolution_bitcast_fusion.9), channel_id=1, replica_groups=mesh['gz'=2,'gy'=4,'gx'=4] {'gz','gy','gx'}, use_global_device_ids=true, to_apply=%region_4.8 | all-reduce | flops 4096 | bytes 32768 | tf_op jit(solution)/shard_map/psum | solution.py:127
  186.6 4.2 %collective-permute-start.15 = (f32[64,1,8,128]{3,0,2,1:T(8,128)S(1)}, f32[64,1,8,128]{3,0,2,1:T(8,128)S(1)}, u32[]{:S(2)}, u32[]{:S(2)}) collective-permute-start(f32[64,1,8,128]{3,0,2,1:T(8,128)S(1)} %fusion.6), channel_id=1, source_target_pairs={{0,16},{1,17},{2,18},{3,19},{4,20},{5,21},{6,22},{7,23},{8,24},{9,... | collective-permute-start | bytes 786440 | tf_op jit(solution)/shard_map/ppermute | solution.py:20
  192.2 3.9 %collective-permute-done.15 = f32[64,1,8,128]{3,0,2,1:T(8,128)S(1)} collective-permute-done((f32[64,1,8,128]{3,0,2,1:T(8,128)S(1)}, f32[64,1,8,128]{3,0,2,1:T(8,128)S(1)}, u32[]{:S(2)}, u32[]{:S(2)}) %collective-permute-start.15) | collective-permute-done | bytes 262176 | tf_op jit(solution)/shard_map/ppermute | solution.py:20
  196.0 4.1 %collective-permute-done.16 = f32[64,1,8,128]{3,0,2,1:T(8,128)S(1)} collective-permute-done((f32[64,1,8,128]{3,0,2,1:T(8,128)S(1)}, f32[64,1,8,128]{3,0,2,1:T(8,128)S(1)}, u32[]{:S(2)}, u32[]{:S(2)}) %collective-permute-start.16) | collective-permute-done | bytes 262176 | tf_op jit(solution)/shard_map/ppermute | solution.py:23
  202.8 2.9 %collective-permute-done.18 = f32[64,3,1,128]{3,0,2,1:T(8,128)S(1)} collective-permute-done((f32[64,3,1,128]{3,0,2,1:T(8,128)S(1)}, f32[64,3,1,128]{3,0,2,1:T(8,128)S(1)}, u32[]{:S(2)}, u32[]{:S(2)}) %collective-permute-start.18) | collective-permute-done | bytes 98336 | tf_op jit(solution)/shard_map/ppermute | solution.py:23
  207.2 3.3 %collective-permute-start.20 = (f32[64,3,10,1]{0,3,2,1:T(1,128)S(1)}, f32[64,3,10,1]{0,3,2,1:T(1,128)S(1)}, u32[]{:S(2)}, u32[]{:S(2)}) collective-permute-start(f32[64,3,10,1]{0,3,2,1:T(1,128)S(1)} %copy.73), channel_id=1, source_target_pairs={{0,1},{1,2},{2,3},{4,5},{5,6},{6,7},{8,9},{9,10},{10,11},{12,13},{... | collective-permute-start | bytes 23048 | tf_op jit(solution)/shard_map/ppermute | solution.py:20
  223.5 40.5 %psum.31 = f32[64,64]{0,1:T(8,128)S(1)} all-reduce(f32[64,64]{0,1:T(8,128)S(1)} %convolution_bitcast_fusion.8), channel_id=1, replica_groups=mesh['gz'=2,'gy'=4,'gx'=4] {'gz','gy','gx'}, use_global_device_ids=true, to_apply=%region_5.9 | all-reduce | flops 4096 | bytes 32768 | tf_op jit(solution)/shard_map/psum | solution.py:122
  264.1 5.8 %cholesky.81 = f32[64,64]{1,0:T(8,128)S(1)} custom-call(f32[64,64]{1,0:T(8,128)S(1)} %fusion.39), custom_call_target="Cholesky" | custom-call | tf_op jit(solution)/shard_map/jit(cholesky)/cholesky | solution.py:92
  271.3 4.9 %custom-call.17 = f32[1,64,64]{1,2,0:T(8,128)S(1)} custom-call(f32[1,64,64]{2,1,0:T(8,128)S(1)} %fusion.35), custom_call_target="InvertDiagBlocksLowerTriangular" | custom-call | tf_op jit(solution)/shard_map/triangular_solve/custom-call.2 | solution.py:94
  (156 shorter events, 67.9 us)
Async XLA Ops:
  1.7 18.6 %collective-permute-start.3 = (f32[64,1,8,128]{3,0,2,1:T(8,128)S(1)}, f32[64,1,8,128]{3,0,2,1:T(8,128)S(1)}, u32[]{:S(2)}, u32[]{:S(2)}) collective-permute-start(f32[64,1,8,128]{3,0,2,1:T(8,128)S(1)} %copy.64), channel_id=1, source_target_pairs={{0,16},{1,17},{2,18},{3,19},{4,20},{5,21},{6,22},{7,23},{8,24},{9,... | collective-permute-start | bytes 786440 | tf_op jit(solution)/shard_map/ppermute | solution.py:20
  6.6 13.8 %collective-permute-start.4 = (f32[64,1,8,128]{3,0,2,1:T(8,128)S(1)}, f32[64,1,8,128]{3,0,2,1:T(8,128)S(1)}, u32[]{:S(2)}, u32[]{:S(2)}) collective-permute-start(f32[64,1,8,128]{3,0,2,1:T(8,128)S(1)} %copy.64), channel_id=1, source_target_pairs={{16,0},{17,1},{18,2},{19,3},{20,4},{21,5},{22,6},{23,7},{24,8},{25... | collective-permute-start | bytes 786440 | tf_op jit(solution)/shard_map/ppermute | solution.py:23
  10.0 15.9 %collective-permute-start = (f32[6,1,8,128]{3,2,1,0:T(8,128)S(1)}, f32[6,1,8,128]{3,2,1,0:T(8,128)S(1)}, u32[]{:S(2)}, u32[]{:S(2)}) collective-permute-start(f32[6,1,8,128]{3,2,1,0:T(8,128)S(1)} %select_add_fusion), channel_id=1, source_target_pairs={{0,16},{1,17},{2,18},{3,19},{4,20},{5,21},{6,22},{7,23},{8,24},{9,... | collective-permute-start | bytes 73736 | tf_op jit(solution)/shard_map/ppermute | solution.py:12
  14.6 11.2 %collective-permute-start.2 = (f32[6,1,8,1]{3,2,1,0:T(8,128)S(1)}, f32[6,1,8,1]{3,2,1,0:T(8,128)S(1)}, u32[]{:S(2)}, u32[]{:S(2)}) collective-permute-start(f32[6,1,8,1]{3,2,1,0:T(8,128)S(1)} %slice.282), channel_id=1, source_target_pairs={{0,1},{1,2},{2,3},{4,5},{5,6},{6,7},{8,9},{9,10},{10,11},{12,13},{... | collective-permute-start | bytes 584 | tf_op jit(solution)/shard_map/ppermute | solution.py:12
  18.1 7.8 %collective-permute-start.1 = (f32[6,1,1,128]{3,2,1,0:T(1,128)S(1)}, f32[6,1,1,128]{3,2,1,0:T(1,128)S(1)}, u32[]{:S(2)}, u32[]{:S(2)}) collective-permute-start(f32[6,1,1,128]{3,2,1,0:T(1,128)S(1)} %slice.281), channel_id=1, source_target_pairs={{0,4},{4,8},{8,12},{1,5},{5,9},{9,13},{2,6},{6,10},{10,14},{3,7},{... | collective-permute-start | bytes 9224 | tf_op jit(solution)/shard_map/ppermute | solution.py:12
  20.4 5.6 %collective-permute-start.5 = (f32[64,3,1,128]{3,0,2,1:T(8,128)S(1)}, f32[64,3,1,128]{3,0,2,1:T(8,128)S(1)}, u32[]{:S(2)}, u32[]{:S(2)}) collective-permute-start(f32[64,3,1,128]{3,0,2,1:T(8,128)S(1)} %get-tuple-element.43), channel_id=1, source_target_pairs={{0,4},{4,8},{8,12},{1,5},{5,9},{9,13},{2,6},{6,10},{10,14},{3,7},{... | collective-permute-start | bytes 294920 | tf_op jit(solution)/shard_map/ppermute | solution.py:20
  24.6 3.2 %collective-permute-start.6 = (f32[64,3,1,128]{3,0,2,1:T(8,128)S(1)}, f32[64,3,1,128]{3,0,2,1:T(8,128)S(1)}, u32[]{:S(2)}, u32[]{:S(2)}) collective-permute-start(f32[64,3,1,128]{3,0,2,1:T(8,128)S(1)} %get-tuple-element.44), channel_id=1, source_target_pairs={{4,0},{8,4},{12,8},{5,1},{9,5},{13,9},{6,2},{10,6},{14,10},{7,3},{... | collective-permute-start | bytes 294920 | tf_op jit(solution)/shard_map/ppermute | solution.py:23
  29.2 5.8 %collective-permute-start.8 = (f32[64,3,10,1]{0,3,2,1:T(1,128)}, f32[64,3,10,1]{0,3,2,1:T(1,128)S(1)}, u32[]{:S(2)}, u32[]{:S(2)}) collective-permute-start(f32[64,3,10,1]{0,3,2,1:T(1,128)} %copy.52), channel_id=1, source_target_pairs={{0,1},{1,2},{2,3},{4,5},{5,6},{6,7},{8,9},{9,10},{10,11},{12,13},{... | collective-permute-start | bytes 23048 | tf_op jit(solution)/shard_map/ppermute | solution.py:20
  33.3 43.5 %copy-start.3 = (f32[2,9,129]{2,1,0:T(8,128)}, f32[2,9,129]{2,1,0:T(8,128)S(1)}, u32[]{:S(2)}) copy-start(f32[2,9,129]{2,1,0:T(8,128)S(1)} %get-tuple-element.50) | copy-start | bytes 27868
  33.6 5.6 %collective-permute-start.7 = (f32[64,3,10,1]{0,3,2,1:T(1,128)S(1)}, f32[64,3,10,1]{0,3,2,1:T(1,128)S(1)}, u32[]{:S(2)}, u32[]{:S(2)}) collective-permute-start(f32[64,3,10,1]{0,3,2,1:T(1,128)S(1)} %copy.50), channel_id=1, source_target_pairs={{1,0},{2,1},{3,2},{5,4},{6,5},{7,6},{9,8},{10,9},{11,10},{13,12},{... | collective-permute-start | bytes 23048 | tf_op jit(solution)/shard_map/ppermute | solution.py:23
  43.2 10.8 %collective-permute-start.10 = (f32[64,1,8,128]{3,0,2,1:T(8,128)S(1)}, f32[64,1,8,128]{3,0,2,1:T(8,128)S(1)}, u32[]{:S(2)}, u32[]{:S(2)}) collective-permute-start(f32[64,1,8,128]{3,0,2,1:T(8,128)S(1)} %fusion.21), channel_id=1, source_target_pairs={{16,0},{17,1},{18,2},{19,3},{20,4},{21,5},{22,6},{23,7},{24,8},{25... | collective-permute-start | bytes 786440 | tf_op jit(solution)/shard_map/ppermute | solution.py:23
  44.5 11.2 %collective-permute-start.9 = (f32[64,1,8,128]{3,0,2,1:T(8,128)S(1)}, f32[64,1,8,128]{3,0,2,1:T(8,128)S(1)}, u32[]{:S(2)}, u32[]{:S(2)}) collective-permute-start(f32[64,1,8,128]{3,0,2,1:T(8,128)S(1)} %fusion.21), channel_id=1, source_target_pairs={{0,16},{1,17},{2,18},{3,19},{4,20},{5,21},{6,22},{7,23},{8,24},{9,... | collective-permute-start | bytes 786440 | tf_op jit(solution)/shard_map/ppermute | solution.py:20
  55.7 3.5 %collective-permute-start.11 = (f32[64,3,1,128]{3,0,2,1:T(8,128)S(1)}, f32[64,3,1,128]{3,0,2,1:T(8,128)S(1)}, u32[]{:S(2)}, u32[]{:S(2)}) collective-permute-start(f32[64,3,1,128]{3,0,2,1:T(8,128)S(1)} %get-tuple-element.41), channel_id=1, source_target_pairs={{0,4},{4,8},{8,12},{1,5},{5,9},{9,13},{2,6},{6,10},{10,14},{3,7},{... | collective-permute-start | bytes 294920 | tf_op jit(solution)/shard_map/ppermute | solution.py:20
  57.9 3.2 %collective-permute-start.12 = (f32[64,3,1,128]{3,0,2,1:T(8,128)S(1)}, f32[64,3,1,128]{3,0,2,1:T(8,128)S(1)}, u32[]{:S(2)}, u32[]{:S(2)}) collective-permute-start(f32[64,3,1,128]{3,0,2,1:T(8,128)S(1)} %get-tuple-element.42), channel_id=1, source_target_pairs={{4,0},{8,4},{12,8},{5,1},{9,5},{13,9},{6,2},{10,6},{14,10},{7,3},{... | collective-permute-start | bytes 294920 | tf_op jit(solution)/shard_map/ppermute | solution.py:23
  61.8 6.8 %collective-permute-start.14 = (f32[64,3,10,1]{0,3,2,1:T(1,128)S(1)}, f32[64,3,10,1]{0,3,2,1:T(1,128)S(1)}, u32[]{:S(2)}, u32[]{:S(2)}) collective-permute-start(f32[64,3,10,1]{0,3,2,1:T(1,128)S(1)} %copy.56), channel_id=1, source_target_pairs={{0,1},{1,2},{2,3},{4,5},{5,6},{6,7},{8,9},{9,10},{10,11},{12,13},{... | collective-permute-start | bytes 23048 | tf_op jit(solution)/shard_map/ppermute | solution.py:20
  67.3 5.9 %collective-permute-start.13 = (f32[64,3,10,1]{0,3,2,1:T(1,128)}, f32[64,3,10,1]{0,3,2,1:T(1,128)}, u32[]{:S(2)}, u32[]{:S(2)}) collective-permute-start(f32[64,3,10,1]{0,3,2,1:T(1,128)} %copy.54), channel_id=1, source_target_pairs={{1,0},{2,1},{3,2},{5,4},{6,5},{7,6},{9,8},{10,9},{11,10},{13,12},{... | collective-permute-start | bytes 23048 | tf_op jit(solution)/shard_map/ppermute | solution.py:23
  186.6 9.4 %collective-permute-start.15 = (f32[64,1,8,128]{3,0,2,1:T(8,128)S(1)}, f32[64,1,8,128]{3,0,2,1:T(8,128)S(1)}, u32[]{:S(2)}, u32[]{:S(2)}) collective-permute-start(f32[64,1,8,128]{3,0,2,1:T(8,128)S(1)} %fusion.6), channel_id=1, source_target_pairs={{0,16},{1,17},{2,18},{3,19},{4,20},{5,21},{6,22},{7,23},{8,24},{9,... | collective-permute-start | bytes 786440 | tf_op jit(solution)/shard_map/ppermute | solution.py:20
  190.9 9.3 %collective-permute-start.16 = (f32[64,1,8,128]{3,0,2,1:T(8,128)S(1)}, f32[64,1,8,128]{3,0,2,1:T(8,128)S(1)}, u32[]{:S(2)}, u32[]{:S(2)}) collective-permute-start(f32[64,1,8,128]{3,0,2,1:T(8,128)S(1)} %fusion.6), channel_id=1, source_target_pairs={{16,0},{17,1},{18,2},{19,3},{20,4},{21,5},{22,6},{23,7},{24,8},{25... | collective-permute-start | bytes 786440 | tf_op jit(solution)/shard_map/ppermute | solution.py:23
  200.2 2.6 collective-permute-start.17
  201.5 4.3 %collective-permute-start.18 = (f32[64,3,1,128]{3,0,2,1:T(8,128)S(1)}, f32[64,3,1,128]{3,0,2,1:T(8,128)S(1)}, u32[]{:S(2)}, u32[]{:S(2)}) collective-permute-start(f32[64,3,1,128]{3,0,2,1:T(8,128)S(1)} %get-tuple-element.40), channel_id=1, source_target_pairs={{4,0},{8,4},{12,8},{5,1},{9,5},{13,9},{6,2},{10,6},{14,10},{7,3},{... | collective-permute-start | bytes 294920 | tf_op jit(solution)/shard_map/ppermute | solution.py:23
  207.2 6.4 %collective-permute-start.20 = (f32[64,3,10,1]{0,3,2,1:T(1,128)S(1)}, f32[64,3,10,1]{0,3,2,1:T(1,128)S(1)}, u32[]{:S(2)}, u32[]{:S(2)}) collective-permute-start(f32[64,3,10,1]{0,3,2,1:T(1,128)S(1)} %copy.73), channel_id=1, source_target_pairs={{0,1},{1,2},{2,3},{4,5},{5,6},{6,7},{8,9},{9,10},{10,11},{12,13},{... | collective-permute-start | bytes 23048 | tf_op jit(solution)/shard_map/ppermute | solution.py:20
  212.3 5.9 %collective-permute-start.19 = (f32[64,3,10,1]{0,3,2,1:T(1,128)}, f32[64,3,10,1]{0,3,2,1:T(1,128)}, u32[]{:S(2)}, u32[]{:S(2)}) collective-permute-start(f32[64,3,10,1]{0,3,2,1:T(1,128)} %copy.71), channel_id=1, source_target_pairs={{1,0},{2,1},{3,2},{5,4},{6,5},{7,6},{9,8},{10,9},{11,10},{13,12},{... | collective-permute-start | bytes 23048 | tf_op jit(solution)/shard_map/ppermute | solution.py:23
  222.6 53.6 %copy-start.21 = (f32[64,64]{1,0:T(8,128)S(1)}, f32[64,64]{1,0:T(8,128)}, u32[]{:S(2)}) copy-start(f32[64,64]{1,0:T(8,128)} %copy-done.20) | copy-start | bytes 49156
  223.4 54.6 %copy-start.5 = (f32[64,1,8,128]{3,2,0,1:T(8,128)S(1)}, f32[64,1,8,128]{3,2,0,1:T(8,128)}, u32[]{:S(2)}) copy-start(f32[64,1,8,128]{3,2,0,1:T(8,128)} %copy.77) | copy-start | bytes 786436
  (20 other events, 159.4 us)
where the time goes:
time: 281 us; the launch traced here: 280 us
  blocking collectives  122 us (43%)
  starting transfers between devices  52.4 us (19%)
  other arithmetic  50.7 us (18%)
  waiting for transfers between devices  25.3 us (9%)
  local copies, waits for them, and re-layouts  22.4 us (8%)
  matrix products  5.49 us (2%)
    psum x1, blocking collectives, body(): rr_now = lax.psum(gram_of(residual, residual), ('gz', 'gy', 'gx'))  42.6 us
    psum x1, blocking collectives, body(): curve = lax.psum(gram_of(direction, image), ('gz', 'gy', 'gx'))  40.5 us
    psum x1, blocking collectives, body(): rr_next = lax.psum(gram_of(residual, residual), ('gz', 'gy', 'gx'))  38.9 us
    ppermute x9, starting transfers between devices, padded_2(): lax.ppermute(lax.slice_in_dim(block, block.shape[dim] - width, None, axis...  31.5 us
    ppermute x9, waiting for transfers between devices, padded_2(): lax.ppermute(lax.slice_in_dim(block, 0, width, axis=dim), axis, backward)  19.7 us
    another operation x9, other arithmetic, factor_solve(): factor = jnp.linalg.cholesky(matrix)  19.6 us
    another operation x6, other arithmetic, factor_solve(): lax.linalg.triangular_solve(factor, halfway, left_side=True, lower=True,...  16.6 us
    ppermute x9, starting transfers between devices, padded_2(): lax.ppermute(lax.slice_in_dim(block, 0, width, axis=dim), axis, backward)  11.6 us
  transfers between devices with their start and end apart: 21, of which 10 were waited for; matrix products, arithmetic and copies ran while one was open for 6% of the time, Pallas kernels for 0%

commit v1 on v0

--- a/solution.py
+++ b/solution.py
@@ -124,7 +124,9 @@
         solution = solution + combine_rows(step_coef, direction)
         residual = residual - combine_rows(step_coef, image)
         if iteration + 1 < ITERS:
-            rr_next = lax.psum(gram_of(residual, residual), ("gz", "gy", "gx"))
+            rr_next = gram_of(residual, residual)
+            for at in (("gy", "gx"), "gz"):
+                rr_next = lax.psum(rr_next, axis_name=at)
             beta_coef = factor_solve(rr_now, rr_next)
             direction = residual + combine_rows(beta_coef, direction)
             rr_now = rr_next

time: 281 us -> 306 us (1.089)
  blocking collectives: 122 us -> 151 us
  starting transfers between devices: 52.4 us -> 48.6 us
    psum x1 -> x2, blocking collectives: 38.9 us -> 67.6 us  [body(): rr_next = lax.psum(rr_next, axis_name=at)]
    ppermute x9, starting transfers between devices: 31.5 us -> 27.7 us  [padded_2(): lax.ppermute(lax.slice_in_dim(block, block.shape[dim] - width, None, axis...]
where the time goes in v1:
time: 306 us; the launch traced here: 305 us
  blocking collectives  151 us (49%)
  other arithmetic  50.7 us (17%)
  starting transfers between devices  48.6 us (16%)
  waiting for transfers between devices  25.5 us (8%)
  local copies, waits for them, and re-layouts  22.4 us (7%)
  matrix products  5.49 us (2%)
    psum x2, blocking collectives, body(): rr_next = lax.psum(rr_next, axis_name=at)  67.6 us
    psum x1, blocking collectives, body(): rr_now = lax.psum(gram_of(residual, residual), ('gz', 'gy', 'gx'))  42.6 us
    psum x1, blocking collectives, body(): curve = lax.psum(gram_of(direction, image), ('gz', 'gy', 'gx'))  40.4 us
    ppermute x9, starting transfers between devices, padded_2(): lax.ppermute(lax.slice_in_dim(block, block.shape[dim] - width, None, axis...  27.7 us
    ppermute x9, waiting for transfers between devices, padded_2(): lax.ppermute(lax.slice_in_dim(block, 0, width, axis=dim), axis, backward)  21.2 us
    another operation x9, other arithmetic, factor_solve(): factor = jnp.linalg.cholesky(matrix)  19.6 us
    another operation x6, other arithmetic, factor_solve(): lax.linalg.triangular_solve(factor, halfway, left_side=True, lower=True,...  16.6 us
    ppermute x9, starting transfers between devices, padded_2(): lax.ppermute(lax.slice_in_dim(block, 0, width, axis=dim), axis, backward)  11.6 us
  transfers between devices with their start and end apart: 21, of which 10 were waited for; matrix products, arithmetic and copies ran while one was open for 6% of the time, Pallas kernels for 0%

profile of v1, /device:TPU:0, one launch (start us, length us, event | category | flops | bytes accessed | tf_op | source)
XLA Modules:
  0.0 304.7 jit_solution(1585819785310053116)
XLA Ops:
  1.7 4.9 %collective-permute-start.3 = (f32[64,1,8,128]{3,0,2,1:T(8,128)S(1)}, f32[64,1,8,128]{3,0,2,1:T(8,128)S(1)}, u32[]{:S(2)}, u32[]{:S(2)}) collective-permute-start(f32[64,1,8,128]{3,0,2,1:T(8,128)S(1)} %copy.64), channel_id=1, source_target_pairs={{0,16},{1,17},{2,18},{3,19},{4,20},{5,21},{6,22},{7,23},{8,24},{9,... | collective-permute-start | bytes 786440 | tf_op jit(solution)/shard_map/ppermute | solution.py:20
  10.0 4.6 %collective-permute-start = (f32[6,1,8,128]{3,2,1,0:T(8,128)S(1)}, f32[6,1,8,128]{3,2,1,0:T(8,128)S(1)}, u32[]{:S(2)}, u32[]{:S(2)}) collective-permute-start(f32[6,1,8,128]{3,2,1,0:T(8,128)S(1)} %select_add_fusion), channel_id=1, source_target_pairs={{0,16},{1,17},{2,18},{3,19},{4,20},{5,21},{6,22},{7,23},{8,24},{9,... | collective-permute-start | bytes 73736 | tf_op jit(solution)/shard_map/ppermute | solution.py:12
  14.6 3.5 %collective-permute-start.2 = (f32[6,1,8,1]{3,2,1,0:T(8,128)S(1)}, f32[6,1,8,1]{3,2,1,0:T(8,128)S(1)}, u32[]{:S(2)}, u32[]{:S(2)}) collective-permute-start(f32[6,1,8,1]{3,2,1,0:T(8,128)S(1)} %slice.282), channel_id=1, source_target_pairs={{0,1},{1,2},{2,3},{4,5},{5,6},{6,7},{8,9},{9,10},{10,11},{12,13},{... | collective-permute-start | bytes 584 | tf_op jit(solution)/shard_map/ppermute | solution.py:12
  20.4 4.1 %collective-permute-start.5 = (f32[64,3,1,128]{3,0,2,1:T(8,128)S(1)}, f32[64,3,1,128]{3,0,2,1:T(8,128)S(1)}, u32[]{:S(2)}, u32[]{:S(2)}) collective-permute-start(f32[64,3,1,128]{3,0,2,1:T(8,128)S(1)} %get-tuple-element.43), channel_id=1, source_target_pairs={{0,4},{4,8},{8,12},{1,5},{5,9},{9,13},{2,6},{6,10},{10,14},{3,7},{... | collective-permute-start | bytes 294920 | tf_op jit(solution)/shard_map/ppermute | solution.py:20
  29.2 3.5 %collective-permute-start.8 = (f32[64,3,10,1]{0,3,2,1:T(1,128)}, f32[64,3,10,1]{0,3,2,1:T(1,128)S(1)}, u32[]{:S(2)}, u32[]{:S(2)}) collective-permute-start(f32[64,3,10,1]{0,3,2,1:T(1,128)} %copy.52), channel_id=1, source_target_pairs={{0,1},{1,2},{2,3},{4,5},{5,6},{6,7},{8,9},{9,10},{10,11},{12,13},{... | collective-permute-start | bytes 23048 | tf_op jit(solution)/shard_map/ppermute | solution.py:20
  44.5 4.6 %collective-permute-start.9 = (f32[64,1,8,128]{3,0,2,1:T(8,128)S(1)}, f32[64,1,8,128]{3,0,2,1:T(8,128)S(1)}, u32[]{:S(2)}, u32[]{:S(2)}) collective-permute-start(f32[64,1,8,128]{3,0,2,1:T(8,128)S(1)} %fusion.21), channel_id=1, source_target_pairs={{0,16},{1,17},{2,18},{3,19},{4,20},{5,21},{6,22},{7,23},{8,24},{9,... | collective-permute-start | bytes 786440 | tf_op jit(solution)/shard_map/ppermute | solution.py:20
  49.1 4.9 %collective-permute-done.10 = f32[64,1,8,128]{3,0,2,1:T(8,128)S(1)} collective-permute-done((f32[64,1,8,128]{3,0,2,1:T(8,128)S(1)}, f32[64,1,8,128]{3,0,2,1:T(8,128)S(1)}, u32[]{:S(2)}, u32[]{:S(2)}) %collective-permute-start.10) | collective-permute-done | bytes 262176 | tf_op jit(solution)/shard_map/ppermute | solution.py:23
  55.7 2.2 collective-permute-start.11
  61.8 3.4 %collective-permute-start.14 = (f32[64,3,10,1]{0,3,2,1:T(1,128)S(1)}, f32[64,3,10,1]{0,3,2,1:T(1,128)S(1)}, u32[]{:S(2)}, u32[]{:S(2)}) collective-permute-start(f32[64,3,10,1]{0,3,2,1:T(1,128)S(1)} %copy.56), channel_id=1, source_target_pairs={{0,1},{1,2},{2,3},{4,5},{5,6},{6,7},{8,9},{9,10},{10,11},{12,13},{... | collective-permute-start | bytes 23048 | tf_op jit(solution)/shard_map/ppermute | solution.py:20
  73.3 2.0 copy.55
  78.5 42.6 %all-reduce.2 = (f32[64,64]{0,1:T(8,128)S(1)}, f32[64,64]{0,1:T(8,128)S(1)}) all-reduce(f32[64,64]{0,1:T(8,128)S(1)} %copy-done.22, f32[64,64]{0,1:T(8,128)S(1)} %convolution_bitcast_fusion.11), channel_id=1, replica_groups=mesh['gz'=2,'gy'=4,'gx'=4] {'gz','gy','gx'}, use_global_device_ids=true, to_apply=%region_3.5 | all-reduce | flops 8192 | bytes 65536 | tf_op jit(solution)/shard_map/psum | solution.py:119
  121.3 5.8 %cholesky.70 = f32[64,64]{1,0:T(8,128)S(1)} custom-call(f32[64,64]{1,0:T(8,128)S(1)} %get-tuple-element.61), custom_call_target="Cholesky" | custom-call | tf_op jit(solution)/shard_map/jit(cholesky)/cholesky | solution.py:92
  128.5 4.9 %custom-call.15 = f32[1,64,64]{1,2,0:T(8,128)S(1)} custom-call(f32[1,64,64]{2,1,0:T(8,128)S(1)} %fusion.34), custom_call_target="InvertDiagBlocksLowerTriangular" | custom-call | tf_op jit(solution)/shard_map/triangular_solve/custom-call.2 | solution.py:94
  133.4 5.9 %cholesky.59 = f32[64,64]{1,0:T(8,128)S(1)} custom-call(f32[64,64]{1,0:T(8,128)S(1)} %get-tuple-element.62), custom_call_target="Cholesky" | custom-call | tf_op jit(solution)/shard_map/jit(cholesky)/cholesky | solution.py:92
  140.6 4.9 %custom-call.13 = f32[1,64,64]{1,2,0:T(8,128)S(1)} custom-call(f32[1,64,64]{2,1,0:T(8,128)S(1)} %fusion.33), custom_call_target="InvertDiagBlocksLowerTriangular" | custom-call | tf_op jit(solution)/shard_map/triangular_solve/custom-call.2 | solution.py:94
  146.8 58.7 %psum.37 = f32[64,64]{1,0:T(8,128)S(1)} all-reduce(f32[64,64]{1,0:T(8,128)S(1)} %convolution_bitcast_fusion.9), channel_id=1, replica_groups=mesh['gz'=2,'gy'=4,'gx'=4] {'gy','gx'}, use_global_device_ids=true, to_apply=%region_4.8 | all-reduce | flops 4096 | bytes 32768 | tf_op jit(solution)/shard_map/psum | solution.py:129
  205.5 8.9 %psum.38 = f32[64,64]{1,0:T(8,128)S(1)} all-reduce(f32[64,64]{1,0:T(8,128)S(1)} %psum.37), channel_id=1, replica_groups=mesh['gz'=2,'gy'=4,'gx'=4] {'gz'}, use_global_device_ids=true, to_apply=%region_5.9 | all-reduce | flops 4096 | bytes 32768 | tf_op jit(solution)/shard_map/psum | solution.py:129
  218.7 2.6 collective-permute-done.15
  221.2 4.4 %collective-permute-done.16 = f32[64,1,8,128]{3,0,2,1:T(8,128)S(1)} collective-permute-done((f32[64,1,8,128]{3,0,2,1:T(8,128)S(1)}, f32[64,1,8,128]{3,0,2,1:T(8,128)S(1)}, u32[]{:S(2)}, u32[]{:S(2)}) %collective-permute-start.16) | collective-permute-done | bytes 262176 | tf_op jit(solution)/shard_map/ppermute | solution.py:23
  228.3 4.1 %collective-permute-done.18 = f32[64,3,1,128]{3,0,2,1:T(8,128)S(1)} collective-permute-done((f32[64,3,1,128]{3,0,2,1:T(8,128)S(1)}, f32[64,3,1,128]{3,0,2,1:T(8,128)S(1)}, u32[]{:S(2)}, u32[]{:S(2)}) %collective-permute-start.18) | collective-permute-done | bytes 98336 | tf_op jit(solution)/shard_map/ppermute | solution.py:23
  243.3 2.0 copy.72
  248.6 40.4 %psum.39 = f32[64,64]{0,1:T(8,128)S(1)} all-reduce(f32[64,64]{0,1:T(8,128)S(1)} %convolution_bitcast_fusion.8), channel_id=1, replica_groups=mesh['gz'=2,'gy'=4,'gx'=4] {'gz','gy','gx'}, use_global_device_ids=true, to_apply=%region_6.10 | all-reduce | flops 4096 | bytes 32768 | tf_op jit(solution)/shard_map/psum | solution.py:122
  289.1 5.8 %cholesky.81 = f32[64,64]{1,0:T(8,128)S(1)} custom-call(f32[64,64]{1,0:T(8,128)S(1)} %fusion.39), custom_call_target="Cholesky" | custom-call | tf_op jit(solution)/shard_map/jit(cholesky)/cholesky | solution.py:92
  296.3 4.9 %custom-call.17 = f32[1,64,64]{1,2,0:T(8,128)S(1)} custom-call(f32[1,64,64]{2,1,0:T(8,128)S(1)} %fusion.35), custom_call_target="InvertDiagBlocksLowerTriangular" | custom-call | tf_op jit(solution)/shard_map/triangular_solve/custom-call.2 | solution.py:94
  (157 shorter events, 69.6 us)
Async XLA Ops:
  1.7 18.6 %collective-permute-start.3 = (f32[64,1,8,128]{3,0,2,1:T(8,128)S(1)}, f32[64,1,8,128]{3,0,2,1:T(8,128)S(1)}, u32[]{:S(2)}, u32[]{:S(2)}) collective-permute-start(f32[64,1,8,128]{3,0,2,1:T(8,128)S(1)} %copy.64), channel_id=1, source_target_pairs={{0,16},{1,17},{2,18},{3,19},{4,20},{5,21},{6,22},{7,23},{8,24},{9,... | collective-permute-start | bytes 786440 | tf_op jit(solution)/shard_map/ppermute | solution.py:20
  6.6 13.8 %collective-permute-start.4 = (f32[64,1,8,128]{3,0,2,1:T(8,128)S(1)}, f32[64,1,8,128]{3,0,2,1:T(8,128)S(1)}, u32[]{:S(2)}, u32[]{:S(2)}) collective-permute-start(f32[64,1,8,128]{3,0,2,1:T(8,128)S(1)} %copy.64), channel_id=1, source_target_pairs={{16,0},{17,1},{18,2},{19,3},{20,4},{21,5},{22,6},{23,7},{24,8},{25... | collective-permute-start | bytes 786440 | tf_op jit(solution)/shard_map/ppermute | solution.py:23
  10.0 15.9 %collective-permute-start = (f32[6,1,8,128]{3,2,1,0:T(8,128)S(1)}, f32[6,1,8,128]{3,2,1,0:T(8,128)S(1)}, u32[]{:S(2)}, u32[]{:S(2)}) collective-permute-start(f32[6,1,8,128]{3,2,1,0:T(8,128)S(1)} %select_add_fusion), channel_id=1, source_target_pairs={{0,16},{1,17},{2,18},{3,19},{4,20},{5,21},{6,22},{7,23},{8,24},{9,... | collective-permute-start | bytes 73736 | tf_op jit(solution)/shard_map/ppermute | solution.py:12
  14.6 11.2 %collective-permute-start.2 = (f32[6,1,8,1]{3,2,1,0:T(8,128)S(1)}, f32[6,1,8,1]{3,2,1,0:T(8,128)S(1)}, u32[]{:S(2)}, u32[]{:S(2)}) collective-permute-start(f32[6,1,8,1]{3,2,1,0:T(8,128)S(1)} %slice.282), channel_id=1, source_target_pairs={{0,1},{1,2},{2,3},{4,5},{5,6},{6,7},{8,9},{9,10},{10,11},{12,13},{... | collective-permute-start | bytes 584 | tf_op jit(solution)/shard_map/ppermute | solution.py:12
  18.1 7.8 %collective-permute-start.1 = (f32[6,1,1,128]{3,2,1,0:T(1,128)S(1)}, f32[6,1,1,128]{3,2,1,0:T(1,128)S(1)}, u32[]{:S(2)}, u32[]{:S(2)}) collective-permute-start(f32[6,1,1,128]{3,2,1,0:T(1,128)S(1)} %slice.281), channel_id=1, source_target_pairs={{0,4},{4,8},{8,12},{1,5},{5,9},{9,13},{2,6},{6,10},{10,14},{3,7},{... | collective-permute-start | bytes 9224 | tf_op jit(solution)/shard_map/ppermute | solution.py:12
  20.4 5.6 %collective-permute-start.5 = (f32[64,3,1,128]{3,0,2,1:T(8,128)S(1)}, f32[64,3,1,128]{3,0,2,1:T(8,128)S(1)}, u32[]{:S(2)}, u32[]{:S(2)}) collective-permute-start(f32[64,3,1,128]{3,0,2,1:T(8,128)S(1)} %get-tuple-element.43), channel_id=1, source_target_pairs={{0,4},{4,8},{8,12},{1,5},{5,9},{9,13},{2,6},{6,10},{10,14},{3,7},{... | collective-permute-start | bytes 294920 | tf_op jit(solution)/shard_map/ppermute | solution.py:20
  24.6 3.2 %collective-permute-start.6 = (f32[64,3,1,128]{3,0,2,1:T(8,128)S(1)}, f32[64,3,1,128]{3,0,2,1:T(8,128)S(1)}, u32[]{:S(2)}, u32[]{:S(2)}) collective-permute-start(f32[64,3,1,128]{3,0,2,1:T(8,128)S(1)} %get-tuple-element.44), channel_id=1, source_target_pairs={{4,0},{8,4},{12,8},{5,1},{9,5},{13,9},{6,2},{10,6},{14,10},{7,3},{... | collective-permute-start | bytes 294920 | tf_op jit(solution)/shard_map/ppermute | solution.py:23
  29.2 5.8 %collective-permute-start.8 = (f32[64,3,10,1]{0,3,2,1:T(1,128)}, f32[64,3,10,1]{0,3,2,1:T(1,128)S(1)}, u32[]{:S(2)}, u32[]{:S(2)}) collective-permute-start(f32[64,3,10,1]{0,3,2,1:T(1,128)} %copy.52), channel_id=1, source_target_pairs={{0,1},{1,2},{2,3},{4,5},{5,6},{6,7},{8,9},{9,10},{10,11},{12,13},{... | collective-permute-start | bytes 23048 | tf_op jit(solution)/shard_map/ppermute | solution.py:20
  33.6 5.6 %collective-permute-start.7 = (f32[64,3,10,1]{0,3,2,1:T(1,128)S(1)}, f32[64,3,10,1]{0,3,2,1:T(1,128)S(1)}, u32[]{:S(2)}, u32[]{:S(2)}) collective-permute-start(f32[64,3,10,1]{0,3,2,1:T(1,128)S(1)} %copy.50), channel_id=1, source_target_pairs={{1,0},{2,1},{3,2},{5,4},{6,5},{7,6},{9,8},{10,9},{11,10},{13,12},{... | collective-permute-start | bytes 23048 | tf_op jit(solution)/shard_map/ppermute | solution.py:23
  43.2 10.8 %collective-permute-start.10 = (f32[64,1,8,128]{3,0,2,1:T(8,128)S(1)}, f32[64,1,8,128]{3,0,2,1:T(8,128)S(1)}, u32[]{:S(2)}, u32[]{:S(2)}) collective-permute-start(f32[64,1,8,128]{3,0,2,1:T(8,128)S(1)} %fusion.21), channel_id=1, source_target_pairs={{16,0},{17,1},{18,2},{19,3},{20,4},{21,5},{22,6},{23,7},{24,8},{25... | collective-permute-start | bytes 786440 | tf_op jit(solution)/shard_map/ppermute | solution.py:23
  44.5 11.2 %collective-permute-start.9 = (f32[64,1,8,128]{3,0,2,1:T(8,128)S(1)}, f32[64,1,8,128]{3,0,2,1:T(8,128)S(1)}, u32[]{:S(2)}, u32[]{:S(2)}) collective-permute-start(f32[64,1,8,128]{3,0,2,1:T(8,128)S(1)} %fusion.21), channel_id=1, source_target_pairs={{0,16},{1,17},{2,18},{3,19},{4,20},{5,21},{6,22},{7,23},{8,24},{9,... | collective-permute-start | bytes 786440 | tf_op jit(solution)/shard_map/ppermute | solution.py:20
  55.7 3.5 %collective-permute-start.11 = (f32[64,3,1,128]{3,0,2,1:T(8,128)S(1)}, f32[64,3,1,128]{3,0,2,1:T(8,128)S(1)}, u32[]{:S(2)}, u32[]{:S(2)}) collective-permute-start(f32[64,3,1,128]{3,0,2,1:T(8,128)S(1)} %get-tuple-element.41), channel_id=1, source_target_pairs={{0,4},{4,8},{8,12},{1,5},{5,9},{9,13},{2,6},{6,10},{10,14},{3,7},{... | collective-permute-start | bytes 294920 | tf_op jit(solution)/shard_map/ppermute | solution.py:20
  57.9 3.2 %collective-permute-start.12 = (f32[64,3,1,128]{3,0,2,1:T(8,128)S(1)}, f32[64,3,1,128]{3,0,2,1:T(8,128)S(1)}, u32[]{:S(2)}, u32[]{:S(2)}) collective-permute-start(f32[64,3,1,128]{3,0,2,1:T(8,128)S(1)} %get-tuple-element.42), channel_id=1, source_target_pairs={{4,0},{8,4},{12,8},{5,1},{9,5},{13,9},{6,2},{10,6},{14,10},{7,3},{... | collective-permute-start | bytes 294920 | tf_op jit(solution)/shard_map/ppermute | solution.py:23
  61.8 6.8 %collective-permute-start.14 = (f32[64,3,10,1]{0,3,2,1:T(1,128)S(1)}, f32[64,3,10,1]{0,3,2,1:T(1,128)S(1)}, u32[]{:S(2)}, u32[]{:S(2)}) collective-permute-start(f32[64,3,10,1]{0,3,2,1:T(1,128)S(1)} %copy.56), channel_id=1, source_target_pairs={{0,1},{1,2},{2,3},{4,5},{5,6},{6,7},{8,9},{9,10},{10,11},{12,13},{... | collective-permute-start | bytes 23048 | tf_op jit(solution)/shard_map/ppermute | solution.py:20
  67.4 5.9 %collective-permute-start.13 = (f32[64,3,10,1]{0,3,2,1:T(1,128)}, f32[64,3,10,1]{0,3,2,1:T(1,128)}, u32[]{:S(2)}, u32[]{:S(2)}) collective-permute-start(f32[64,3,10,1]{0,3,2,1:T(1,128)} %copy.54), channel_id=1, source_target_pairs={{1,0},{2,1},{3,2},{5,4},{6,5},{7,6},{9,8},{10,9},{11,10},{13,12},{... | collective-permute-start | bytes 23048 | tf_op jit(solution)/shard_map/ppermute | solution.py:23
  146.0 69.4 %copy-start.18 = (f32[64,64,1]{0,1,2:T(8,128)}, f32[64,64,1]{0,1,2:T(8,128)S(1)}, u32[]{:S(2)}) copy-start(f32[64,64,1]{0,1,2:T(8,128)S(1)} %convolution_bitcast_fusion.7) | copy-start | bytes 49156
  215.4 5.8 %collective-permute-start.15 = (f32[64,1,8,128]{3,0,2,1:T(8,128)S(1)}, f32[64,1,8,128]{3,0,2,1:T(8,128)S(1)}, u32[]{:S(2)}, u32[]{:S(2)}) collective-permute-start(f32[64,1,8,128]{3,0,2,1:T(8,128)S(1)} %fusion.6), channel_id=1, source_target_pairs={{0,16},{1,17},{2,18},{3,19},{4,20},{5,21},{6,22},{7,23},{8,24},{9,... | collective-permute-start | bytes 786440 | tf_op jit(solution)/shard_map/ppermute | solution.py:20
  217.4 8.3 %collective-permute-start.16 = (f32[64,1,8,128]{3,0,2,1:T(8,128)S(1)}, f32[64,1,8,128]{3,0,2,1:T(8,128)S(1)}, u32[]{:S(2)}, u32[]{:S(2)}) collective-permute-start(f32[64,1,8,128]{3,0,2,1:T(8,128)S(1)} %fusion.6), channel_id=1, source_target_pairs={{16,0},{17,1},{18,2},{19,3},{20,4},{21,5},{22,6},{23,7},{24,8},{25... | collective-permute-start | bytes 786440 | tf_op jit(solution)/shard_map/ppermute | solution.py:23
  225.6 2.6 collective-permute-start.17
  227.0 5.5 %collective-permute-start.18 = (f32[64,3,1,128]{3,0,2,1:T(8,128)S(1)}, f32[64,3,1,128]{3,0,2,1:T(8,128)S(1)}, u32[]{:S(2)}, u32[]{:S(2)}) collective-permute-start(f32[64,3,1,128]{3,0,2,1:T(8,128)S(1)} %get-tuple-element.40), channel_id=1, source_target_pairs={{4,0},{8,4},{12,8},{5,1},{9,5},{13,9},{6,2},{10,6},{14,10},{7,3},{... | collective-permute-start | bytes 294920 | tf_op jit(solution)/shard_map/ppermute | solution.py:23
  233.8 4.9 %collective-permute-start.20 = (f32[64,3,10,1]{0,3,2,1:T(1,128)S(1)}, f32[64,3,10,1]{0,3,2,1:T(1,128)S(1)}, u32[]{:S(2)}, u32[]{:S(2)}) collective-permute-start(f32[64,3,10,1]{0,3,2,1:T(1,128)S(1)} %copy.73), channel_id=1, source_target_pairs={{0,1},{1,2},{2,3},{4,5},{5,6},{6,7},{8,9},{9,10},{10,11},{12,13},{... | collective-permute-start | bytes 23048 | tf_op jit(solution)/shard_map/ppermute | solution.py:20
  237.4 5.9 %collective-permute-start.19 = (f32[64,3,10,1]{0,3,2,1:T(1,128)}, f32[64,3,10,1]{0,3,2,1:T(1,128)}, u32[]{:S(2)}, u32[]{:S(2)}) collective-permute-start(f32[64,3,10,1]{0,3,2,1:T(1,128)} %copy.71), channel_id=1, source_target_pairs={{1,0},{2,1},{3,2},{5,4},{6,5},{7,6},{9,8},{10,9},{11,10},{13,12},{... | collective-permute-start | bytes 23048 | tf_op jit(solution)/shard_map/ppermute | solution.py:23
  247.7 53.6 %copy-start.21 = (f32[64,64]{1,0:T(8,128)S(1)}, f32[64,64]{1,0:T(8,128)}, u32[]{:S(2)}) copy-start(f32[64,64]{1,0:T(8,128)} %copy-done.20) | copy-start | bytes 49156
  248.5 54.6 %copy-start.5 = (f32[64,1,8,128]{3,2,0,1:T(8,128)S(1)}, f32[64,1,8,128]{3,2,0,1:T(8,128)}, u32[]{:S(2)}) copy-start(f32[64,1,8,128]{3,2,0,1:T(8,128)} %copy.77) | copy-start | bytes 786436
  (20 other events, 163.5 us)
